TPU v7x, 512 devices: a whole 4x4x16 slice. The times are simulated.
512 devices in a mesh: pipe: 4 (over x), sp: 32 (over z, core), dp: 4 (over y).
Axes of the slice: x: 4, y: 4, z: 16, core: 2. Of those that a mesh axis runs over, the one named last changes fastest.
Arguments:
- fresh_input: bfloat16 [4, 4, 128, 240, 128], P('pipe', 'dp', 'sp'), may hold values from -6 to 6
- saved_input: bfloat16 [4, 4, 128, 240, 128], P('pipe', 'dp', 'sp'), may hold values from -6 to 6
- output_grad: bfloat16 [4, 4, 128, 240, 128], P('pipe', 'dp', 'sp'), may hold values from -6 to 6
- expand_weight: bfloat16 [4, 128, 768], P('pipe'), may hold values from -0.5 to 0.5
- reduce_weight: bfloat16 [4, 768, 128], P('pipe'), may hold values from -0.21875 to 0.21875
- filter_weight: float32 [4, 2, 120, 128], P('pipe'), may hold values from -6 to 6
- cycle_table: int32 [128], replicated, may hold values from 0 to 127, each once
Outputs:
- next_input: bfloat16 [4, 4, 128, 240, 128], P('pipe', 'dp', 'sp')
- input_grad: bfloat16 [4, 4, 128, 240, 128], P('pipe', 'dp', 'sp')
- expand_grad: float32 [4, 128, 768], P('pipe', None, 'dp')
- reduce_grad: float32 [4, 768, 128], P('pipe', 'dp')
- filter_grad: float32 [4, 2, 120, 128], P('pipe')
Inputs may be any that keep to these rules, and one draw needn't show every extreme that they name: `cycle_table`: each of 0 .. 127 appears once; values 120 or more mark empty cycle slots.
All inputs are finite; a program needn't handle non-finite values.
Results may differ from a plain program's by a relative error of at most 0.025.
Values may be sent and summed in bfloat16 or wider, within the bound.
No kernel may reach another device: no remote copies, remote signals or barrier semaphores. Data moves between devices by JAX's collectives and lax.ppermute only.
A program may use at most 64 MiB of HBM per device.

v0:
```python
import math
import jax
import jax.numpy as jnp
from jax import lax
from jax.sharding import Mesh
from jax.sharding import PartitionSpec as P

NLAT = 120
NLON = 240
SP = ("sp_0", "sp_1")
SP_DP = ("sp_0", "sp_1", "dp")
ROOT_HALF = 0.7071067811865476
INV_ROOT_TAU = 0.3989422804014327


def from_behind(block, axis, distance):
    devices = range(lax.axis_size(axis))
    route = [(i - distance, i) for i in devices if i - distance in devices]
    return lax.ppermute(block, axis, route)


def one_axis_at_a_time(shard, axes):
    for axis in axes:
        shard = lax.psum(shard, axis)
    return shard


def in_blocks(shard, dim, peers):
    lengths = shard.shape
    blocks = shard.reshape(*lengths[:dim], peers, lengths[dim] // peers, *lengths[dim + 1 :])
    return jnp.moveaxis(blocks, dim, 0)


def summed_on_arrival(shard, axis, dim):
    blocks = in_blocks(shard, dim, lax.axis_size(axis))
    arrived = lax.all_to_all(blocks, axis, split_axis=0, concat_axis=0, tiled=True)
    return arrived.astype(jnp.float32).sum(axis=0)


def total_of_pieces(shard, axis):
    return lax.all_gather(shard, axis).astype(jnp.float32).sum(0)


def gelu_value(pre_act):
    return 0.5 * pre_act * (1.0 + lax.erf(pre_act * ROOT_HALF))


def gelu_slope(pre_act):
    return (
        0.5 * (1.0 + lax.erf(pre_act * ROOT_HALF))
        + pre_act * jnp.exp(-0.5 * pre_act * pre_act) * INV_ROOT_TAU
    )


def legendre(lat_index, order_index, cycles):
    lat_ok = (lat_index < cycles).astype(jnp.float32)
    order_ok = (order_index < cycles).astype(jnp.float32)
    colatitude = math.pi * (jnp.minimum(lat_index, cycles - 1).astype(jnp.float32) + 0.5) / cycles
    cosine = jnp.cos(colatitude)[None, :]
    sine_value = jnp.sin(colatitude)[None, :]
    order_value = jnp.minimum(order_index, cycles - 1).astype(jnp.float32)[:, None]
    log_start = 0.5 * (
        jnp.log((2.0 * order_value + 1.0) / (4.0 * math.pi))
        + lax.lgamma(2.0 * order_value + 1.0)
        - 2.0 * lax.lgamma(order_value + 1.0)
        - order_value * math.log(4.0)
    ) + order_value * jnp.log(sine_value)
    starting = jnp.exp(log_start)
    zero_rows = jnp.zeros_like(starting)

    def advance(state_pair, degree):
        previous, earlier = state_pair
        degree_value = degree.astype(jnp.float32)
        upper_term = jnp.maximum(4.0 * degree_value * degree_value - 1.0, 0.0)
        ratio_main = jnp.sqrt(
            upper_term / jnp.maximum(degree_value * degree_value - order_value * order_value, 1.0)
        )
        ratio_back = jnp.sqrt(
            jnp.maximum((degree_value - 1.0) ** 2 - order_value * order_value, 0.0)
            / jnp.maximum(4.0 * (degree_value - 1.0) ** 2 - 1.0, 1.0)
        )
        rising = ratio_main * (cosine * previous - ratio_back * earlier)
        current = jnp.where(
            degree_value == order_value,
            starting,
            jnp.where(degree_value > order_value, rising, 0.0),
        )
        return ((current, previous), current)

    _, stacked = lax.scan(advance, (zero_rows, zero_rows), jnp.arange(cycles, dtype=jnp.int32))
    valid_mask = order_ok[:, None] * lat_ok[None, :]
    return jnp.transpose(stacked, (1, 0, 2)) * valid_mask[:, None, :]


def cycle_weights(lat_index, cycles):
    valid_cycle = (lat_index < cycles).astype(jnp.float32)
    colatitude = math.pi * (jnp.minimum(lat_index, cycles - 1).astype(jnp.float32) + 0.5) / cycles
    return math.pi / cycles * jnp.sin(colatitude) * valid_cycle


def fourier_tables(order_index, cycles, points):
    valid_order = (order_index < cycles).astype(jnp.float32)[None, :]
    order_value = jnp.minimum(order_index, cycles - 1)
    longitude = jnp.arange(points, dtype=jnp.int32)
    phase_angle = (
        2.0
        * math.pi
        / points
        * (longitude[:, None] * order_value[None, :] % points).astype(jnp.float32)
    )
    scaled = valid_order * (2.0 * math.pi / points)
    forward = jnp.concatenate(
        [jnp.cos(phase_angle) * scaled, -jnp.sin(phase_angle) * scaled], axis=1
    )
    order_scale = jnp.where(order_value == 0, 1.0, 2.0)[None, :] * valid_order / (2.0 * math.pi)
    inverse = jnp.concatenate(
        [jnp.cos(phase_angle) * order_scale, -jnp.sin(phase_angle) * order_scale], axis=1
    ).T
    return (forward.astype(jnp.bfloat16), inverse.astype(jnp.bfloat16))


def joint_orders(coeffs):
    return lax.all_to_all(coeffs, SP, split_axis=3, concat_axis=1, tiled=True)


def joint_cycles(values):
    return lax.all_to_all(values, SP, split_axis=1, concat_axis=3, tiled=True)


def spectral_pass(tokens, filt, forward, analysis, synthesis, inverse, to_orders, to_cycles):
    batch_count, row_count, points, chan_count = tokens.shape
    order_count = forward.shape[1] // 2
    coeffs = jnp.einsum(
        "sjnc,nk->sjkc", tokens, forward, preferred_element_type=jnp.float32
    ).astype(jnp.bfloat16)
    coeffs = coeffs.reshape(batch_count, row_count, 2, order_count, chan_count)
    arrived = to_orders(coeffs)
    spectra = jnp.einsum("tlj,sjrtc->strlc", analysis, arrived, preferred_element_type=jnp.float32)
    real_part = filt[0] * spectra[:, :, 0] - filt[1] * spectra[:, :, 1]
    imag_part = filt[0] * spectra[:, :, 1] + filt[1] * spectra[:, :, 0]
    filtered = jnp.stack([real_part, imag_part], axis=2).astype(jnp.bfloat16)
    values = jnp.einsum(
        "tlj,strlc->sjrtc", synthesis, filtered, preferred_element_type=jnp.float32
    ).astype(jnp.bfloat16)
    returned = to_cycles(values).reshape(batch_count, row_count, 2 * order_count, chan_count)
    spatial = jnp.einsum("sjkc,kn->sjnc", returned, inverse, preferred_element_type=jnp.float32)
    return (spatial, spectra)


def mlp_pass(tokens, spatial, expand, contract, cycle_mask):
    grid_shape = tokens.shape
    flat_rows = (tokens.astype(jnp.float32) + spatial).reshape(-1, grid_shape[-1])
    mixed_b = flat_rows.astype(jnp.bfloat16)
    hidden_pre = jnp.dot(mixed_b, expand, preferred_element_type=jnp.float32)
    hidden = gelu_value(hidden_pre).astype(jnp.bfloat16)
    result = flat_rows + jnp.dot(hidden, contract, preferred_element_type=jnp.float32)
    result = (result.reshape(grid_shape) * cycle_mask[:, None, None]).astype(jnp.bfloat16)
    return (result, mixed_b, hidden_pre, hidden)


def backward_rows(cotangent, cycle_mask, mixed_b, hidden_pre, hidden, expand, contract):
    chan_count = cotangent.shape[-1]
    masked = (cotangent * cycle_mask.astype(jnp.bfloat16)[:, None, None]).reshape(-1, chan_count)
    grad_reduce = jnp.dot(hidden.T, masked, preferred_element_type=jnp.float32)
    grad_hidden = jnp.dot(masked, contract.T, preferred_element_type=jnp.float32)
    grad_pre = (grad_hidden * gelu_slope(hidden_pre)).astype(jnp.bfloat16)
    grad_expand = jnp.dot(mixed_b.T, grad_pre, preferred_element_type=jnp.float32)
    grad_mixed = masked.astype(jnp.float32) + jnp.dot(
        grad_pre, expand.T, preferred_element_type=jnp.float32
    )
    return (grad_mixed, grad_expand, grad_reduce)


def on_device(
    fresh_input, saved_input, output_grad, expand_weight, reduce_weight, filter_weight, cycle_table
):
    slot_count = fresh_input.shape[2]
    position = lax.axis_index(SP)
    order_table = jnp.arange(slot_count * lax.axis_size(SP), dtype=jnp.int32)
    own_cycles = lax.dynamic_slice_in_dim(cycle_table, position * slot_count, slot_count)
    own_orders = lax.dynamic_slice_in_dim(order_table, position * slot_count, slot_count)
    cycle_mask = (own_cycles < NLAT).astype(jnp.float32)
    table = legendre(cycle_table, own_orders, NLAT)
    analysis = (table * cycle_weights(cycle_table, NLAT)[None, None, :]).astype(jnp.bfloat16)
    synthesis = table.astype(jnp.bfloat16)
    forward, inverse = fourier_tables(order_table, NLAT, NLON)
    filt = filter_weight[0]
    expand = expand_weight[0]
    contract = reduce_weight[0]
    fresh = fresh_input[0, 0]
    saved = saved_input[0, 0]
    spatial, spectra = spectral_pass(
        jnp.stack([fresh, saved]),
        filt,
        forward,
        analysis,
        synthesis,
        inverse,
        joint_orders,
        joint_cycles,
    )
    fresh_spatial = spatial[0]
    saved_spatial = spatial[1]
    saved_spectra = spectra[1]
    block = mlp_pass(fresh, fresh_spatial, expand, contract, cycle_mask)[0]
    next_input = from_behind(block[None, None], "pipe", 1)
    _, mixed_b, hidden_pre, hidden = mlp_pass(saved, saved_spatial, expand, contract, cycle_mask)
    grad_mixed, grad_expand, grad_reduce = backward_rows(
        output_grad[0, 0], cycle_mask, mixed_b, hidden_pre, hidden, expand, contract
    )
    grid_shape = saved.shape
    row_count, points, chan_count = grid_shape
    order_count = forward.shape[1] // 2
    grad_rows = grad_mixed.reshape(grid_shape).astype(jnp.bfloat16)
    grad_values = jnp.einsum(
        "jnc,kn->jkc", grad_rows, inverse, preferred_element_type=jnp.float32
    ).astype(jnp.bfloat16)
    grad_values = grad_values.reshape(row_count, 2, order_count, chan_count)
    arrived = lax.all_to_all(grad_values, SP, split_axis=2, concat_axis=0, tiled=True)
    grad_filtered = jnp.einsum(
        "tlj,jrtc->trlc", synthesis, arrived, preferred_element_type=jnp.float32
    )
    filter_real = jnp.sum(
        grad_filtered[:, 0] * saved_spectra[:, 0] + grad_filtered[:, 1] * saved_spectra[:, 1],
        axis=0,
    )
    filter_imag = jnp.sum(
        grad_filtered[:, 1] * saved_spectra[:, 0] - grad_filtered[:, 0] * saved_spectra[:, 1],
        axis=0,
    )
    grad_spectra = jnp.stack(
        [
            filt[0] * grad_filtered[:, 0] + filt[1] * grad_filtered[:, 1],
            filt[0] * grad_filtered[:, 1] - filt[1] * grad_filtered[:, 0],
        ],
        axis=1,
    ).astype(jnp.bfloat16)
    grad_coeffs = jnp.einsum(
        "tlj,trlc->jrtc", analysis, grad_spectra, preferred_element_type=jnp.float32
    ).astype(jnp.bfloat16)
    returned = lax.all_to_all(grad_coeffs, SP, split_axis=0, concat_axis=2, tiled=True)
    grad_tokens = jnp.einsum(
        "jkc,nk->jnc",
        returned.reshape(row_count, 2 * order_count, chan_count),
        forward,
        preferred_element_type=jnp.float32,
    )
    input_grad = (
        (grad_mixed.reshape(grid_shape) + grad_tokens) * cycle_mask[:, None, None]
    ).astype(jnp.bfloat16)
    sent_back = from_behind(input_grad[None, None], "pipe", -1)
    filter_grad = one_axis_at_a_time(jnp.stack([filter_real, filter_imag]), SP_DP)
    shares = (
        summed_on_arrival(grad_expand.astype(jnp.bfloat16), "dp", 1),
        summed_on_arrival(grad_reduce.astype(jnp.bfloat16), "dp", 0),
    )
    expand_grad, reduce_grad = (
        total_of_pieces(shares[0].astype(jnp.bfloat16), SP).astype(jnp.float32),
        total_of_pieces(shares[1].astype(jnp.bfloat16), SP).astype(jnp.float32),
    )
    return (next_input, sent_back, expand_grad[None], reduce_grad[None], filter_grad[None])


def solution(mesh):
    finer = Mesh(
        mesh.devices.reshape(mesh.shape["pipe"], 16, 2, mesh.shape["dp"]),
        ("pipe", "sp_0", "sp_1", "dp"),
    )
    in_specs = (
        P("pipe", "dp", SP, None, None),
        P("pipe", "dp", SP, None, None),
        P("pipe", "dp", SP, None, None),
        P("pipe", None, None),
        P("pipe", None, None),
        P("pipe", None, None, None),
        P(),
    )
    out_specs = (
        P("pipe", "dp", SP, None, None),
        P("pipe", "dp", SP, None, None),
        P("pipe", None, "dp"),
        P("pipe", "dp", None),
        P("pipe", None, None, None),
    )
    return jax.shard_map(
        on_device, mesh=finer, in_specs=in_specs, out_specs=out_specs, check_vma=False
    )
```

profile of v0, /device:TPU:1, one launch (start us, length us, event | category | flops | bytes accessed | tf_op | source)
XLA Modules:
  0.0 563.0 jit_solution(15364229615342538682)
XLA Ops:
  9.2 1.4 convolution_convert_fusion.1
  10.6 1.3 copy.46
  12.0 16.7 %all-to-all-start = ((bf16[2,4,2,128,128]{4,2,1,0,3:T(2,128)(2,1)}), bf16[2,4,2,128,128]{4,2,1,0,3:T(2,128)(2,1)S(1)}, u32[]{:S(2)}, u32[]{:S(2)}) async-start(bf16[2,4,2,128,128]{4,2,1,0,3:T(2,128)(2,1)} %copy.46), calls=%async_computation | async-start | bytes 1048576 | tf_op jit(solution)/shard_map/all_to_all | solution.py:123
  29.0 164.7 %while.18 = (s32[]{:T(128)}, f32[4,128]{1,0:T(4,128)S(1)}, f32[4,128]{1,0:T(4,128)S(1)}, f32[120,4,128]{2,1,0:T(4,128)S(1)}, s32[120]{0:T(128)S(1)}, /*index=5*/...) while((s32[]{:T(128)}, f32[4,128]{1,0:T(4,128)S(1)}, ...), condition=%wide.region_1.2_spmd.clone, body=%wide.region_0.1_spmd.clone.sunk | while | flops 4654 | bytes 14747 | solution.py:90
  41.4 0.6 dynamic_slice.23
  46.9 0.6 dynamic_slice.23
  67.4 0.6 dynamic_slice.23
  72.9 0.6 dynamic_slice.23
  93.5 0.6 dynamic_slice.23
  99.0 0.6 dynamic_slice.23
  193.9 0.8 fusion.54
  195.7 1.1 copy.50
  196.8 12.3 %all-to-all-start.1 = ((bf16[2,128,2,4,128]{4,2,0,3,1:T(2,128)(2,1)}), bf16[2,128,2,4,128]{4,2,0,3,1:T(2,128)(2,1)S(1)}, u32[]{:S(2)}, u32[]{:S(2)}) async-start(bf16[2,128,2,4,128]{4,2,0,3,1:T(2,128)(2,1)} %copy.50), calls=%async_computation.1 | async-start | bytes 1048576 | tf_op jit(solution)/shard_map/all_to_all | solution.py:127
  209.3 0.8 broadcast_multiply_fusion
  210.3 32.4 %all-to-all-done.1 = bf16[2,128,2,4,128]{4,2,0,3,1:T(2,128)(2,1)S(1)} async-done(((bf16[2,128,2,4,128]{4,2,0,3,1:T(2,128)(2,1)}), bf16[2,128,2,4,128]{4,2,0,3,1:T(2,128)(2,1)S(1)}, u32[]{:S(2)}, u32[]{:S(2)}) %all-to-all-start.1) | async-done | bytes 524320 | tf_op jit(solution)/shard_map/all_to_all | solution.py:127
  243.6 1.1 fusion.76
  245.2 1.4 fusion.7
  247.6 1.0 copy.53
  248.6 4.0 all-to-all-start.2
  252.6 0.8 slice_bitcast_fusion
  253.5 1.8 fusion.25
  255.3 19.3 %all-to-all-done.2 = bf16[4,2,128,128]{3,1,0,2:T(2,128)(2,1)S(1)} async-done(((bf16[4,2,128,128]{3,1,0,2:T(2,128)(2,1)}), bf16[4,2,128,128]{3,1,0,2:T(2,128)(2,1)S(1)}, u32[]{:S(2)}, u32[]{:S(2)}) %all-to-all-start.2) | async-done | bytes 262176 | tf_op jit(solution)/shard_map/all_to_all | solution.py:219
  274.7 1.2 convolution_bitcast_fusion.3
  275.8 1.2 add_reduce_fusion
  277.1 0.7 pad_maximum_fusion.2
  277.7 1.3 convolution_convert_fusion.4
  279.1 0.8 copy.60
  279.9 4.3 all-to-all-start.4
  284.2 110.5 %all-reduce.4.cloned.1.call-done = f32[2,120,128]{2,1,0:T(8,128)} async-done(((f32[2,120,128]{2,1,0:T(8,128)}), f32[2,120,128]{2,1,0:T(8,128)}) %all-reduce.4.cloned.1.call-update) | async-done | bytes 122896 | tf_op jit(solution)/shard_map/psum | solution.py:24
  394.9 0.7 reduce_sum.60
  395.7 2.7 fusion.16
  398.4 9.0 %all_to_all.76 = bf16[4,192,128]{2,1,0:T(8,128)(2,1)S(1)} all-to-all(bf16[4,192,128]{2,1,0:T(8,128)(2,1)S(1)} %bitcast.190), channel_id=1, replica_groups=mesh['pipe'=4,'sp_0'=16,'sp_1'=2,'dp'=4] {'dp'}, dimensions={0} | all-to-all | bytes 393216 | tf_op jit(solution)/shard_map/all_to_all | solution.py:36
  407.4 0.7 reduce_sum.62
  408.4 0.9 copy.57
  409.2 18.6 %all-to-all-start.3 = ((bf16[128,2,4,128]{3,1,2,0:T(2,128)(2,1)}), bf16[128,2,4,128]{3,1,2,0:T(2,128)(2,1)S(1)}, u32[]{:S(2)}, u32[]{:S(2)}) async-start(bf16[128,2,4,128]{3,1,2,0:T(2,128)(2,1)} %copy.57), calls=%async_computation.3 | async-start | bytes 524288 | tf_op jit(solution)/shard_map/all_to_all | solution.py:241
  428.2 1.0 fusion.14
  429.3 3.1 collective-permute-start
  432.4 19.4 %all-to-all-done.3 = bf16[128,2,4,128]{3,1,2,0:T(2,128)(2,1)S(1)} async-done(((bf16[128,2,4,128]{3,1,2,0:T(2,128)(2,1)}), bf16[128,2,4,128]{3,1,2,0:T(2,128)(2,1)S(1)}, u32[]{:S(2)}, u32[]{:S(2)}) %all-to-all-start.3) | async-done | bytes 262176 | tf_op jit(solution)/shard_map/all_to_all | solution.py:241
  452.3 1.3 collective-permute-start.1
  453.7 7.5 %collective-permute-done.1 = bf16[1,1,4,240,128]{4,3,2,1,0:T(8,128)(2,1)S(1)} collective-permute-done((bf16[1,1,4,240,128]{4,3,2,1,0:T(8,128)(2,1)S(1)}, bf16[1,1,4,240,128]{4,3,2,1,0:T(8,128)(2,1)S(1)}, u32[]{:S(2)}, u32[]{:S(2)}) %collective-permute-start.1) | collective-permute-done | bytes 245792 | tf_op jit(solution)/shard_map/ppermute | solution.py:19
  461.2 21.4 %all-gather.5.cloned.1.call-done = bf16[4096,192]{0,1:T(8,128)(2,1)} async-done(((bf16[128,192]{0,1:T(8,128)(2,1)}), bf16[4096,192]{0,1:T(8,128)(2,1)}) %all-gather.5.cloned.1.call-update) | async-done | bytes 1572880 | tf_op jit(solution)/shard_map/all_gather | solution.py:41
  482.6 1.7 convert_bitcast_fusion
  484.9 1.1 bitcast_reduce_fusion
  486.0 64.7 %all-gather.7.cloned.1.call-done = bf16[6144,128]{1,0:T(8,128)(2,1)} async-done(((bf16[192,128]{1,0:T(8,128)(2,1)}), bf16[6144,128]{1,0:T(8,128)(2,1)}) %all-gather.7.cloned.1.call-update) | async-done | bytes 1572880 | tf_op jit(solution)/shard_map/all_gather | solution.py:41
  550.7 2.3 convert_reduce_fusion
  553.0 0.7 copy.102
  553.7 0.7 copy.103
  554.4 1.6 copy.104
  (572 shorter events, 87.4 us)
Async XLA Ops:
  8.0 236.7 %copy-start = (bf16[1,128,768]{2,1,0:T(8,128)(2,1)S(1)}, bf16[1,128,768]{2,1,0:T(8,128)(2,1)}, u32[]{:S(2)}) copy-start(bf16[1,128,768]{2,1,0:T(8,128)(2,1)} %param.12) | copy-start | bytes 589828
  8.0 20.9 %copy-start.21 = (s32[128]{0:T(128)S(1)}, s32[128]{0:T(128)}, u32[]{:S(2)}) copy-start(s32[128]{0:T(128)} %param.15) | copy-start | bytes 1540
  8.0 185.8 %copy-start.20 = (f32[1,2,120,128]{3,2,1,0:T(8,128)S(1)}, f32[1,2,120,128]{3,2,1,0:T(8,128)}, u32[]{:S(2)}) copy-start(f32[1,2,120,128]{3,2,1,0:T(8,128)} %param.14) | copy-start | bytes 368644
  8.6 0.6 copy-start.16
  8.6 2.0 copy-start.18
  8.6 234.6 %copy-start.6 = (bf16[240,128]{1,0:T(8,128)(2,1)}, bf16[240,128]{1,0:T(8,128)(2,1)S(1)}, u32[]{:S(2)}) copy-start(bf16[240,128]{1,0:T(8,128)(2,1)S(1)} %get-tuple-element.233) | copy-start | bytes 184324
  8.6 234.6 %copy-start.8 = (bf16[240,128]{1,0:T(8,128)(2,1)}, bf16[240,128]{1,0:T(8,128)(2,1)S(1)}, u32[]{:S(2)}) copy-start(bf16[240,128]{1,0:T(8,128)(2,1)S(1)} %get-tuple-element.234) | copy-start | bytes 184324
  12.0 182.7 %all-to-all-start = ((bf16[2,4,2,128,128]{4,2,1,0,3:T(2,128)(2,1)}), bf16[2,4,2,128,128]{4,2,1,0,3:T(2,128)(2,1)S(1)}, u32[]{:S(2)}, u32[]{:S(2)}) async-start(bf16[2,4,2,128,128]{4,2,1,0,3:T(2,128)(2,1)} %copy.46), calls=%async_computation | async-start | bytes 1048576 | tf_op jit(solution)/shard_map/all_to_all | solution.py:123
  194.9 14.4 %copy-start.2 = (bf16[1,1,4,240,128]{4,3,2,1,0:T(8,128)(2,1)S(1)}, bf16[1,1,4,240,128]{4,3,2,1,0:T(8,128)(2,1)}, u32[]{:S(2)}) copy-start(bf16[1,1,4,240,128]{4,3,2,1,0:T(8,128)(2,1)} %param.11) | copy-start | bytes 737284
  196.8 46.7 %copy-start.5 = (bf16[1,1,4,240,128]{4,3,2,1,0:T(8,128)(2,1)S(1)}, bf16[1,1,4,240,128]{4,3,2,1,0:T(8,128)(2,1)}, u32[]{:S(2)}) copy-start(bf16[1,1,4,240,128]{4,3,2,1,0:T(8,128)(2,1)} %param.10) | copy-start | bytes 737284
  196.8 46.7 %copy-start.13 = (bf16[1,1,4,240,128]{4,3,2,1,0:T(8,128)(2,1)S(1)}, bf16[1,1,4,240,128]{4,3,2,1,0:T(8,128)(2,1)}, u32[]{:S(2)}) copy-start(bf16[1,1,4,240,128]{4,3,2,1,0:T(8,128)(2,1)} %param.9) | copy-start | bytes 737284
  196.8 45.8 %all-to-all-start.1 = ((bf16[2,128,2,4,128]{4,2,0,3,1:T(2,128)(2,1)}), bf16[2,128,2,4,128]{4,2,0,3,1:T(2,128)(2,1)S(1)}, u32[]{:S(2)}, u32[]{:S(2)}) async-start(bf16[2,128,2,4,128]{4,2,0,3,1:T(2,128)(2,1)} %copy.50), calls=%async_computation.1 | async-start | bytes 1048576 | tf_op jit(solution)/shard_map/all_to_all | solution.py:127
  210.3 36.4 %copy-start.3 = (bf16[960,128]{1,0:T(8,128)(2,1)}, bf16[960,128]{1,0:T(8,128)(2,1)S(1)}, u32[]{:S(2)}) copy-start(bf16[960,128]{1,0:T(8,128)(2,1)S(1)} %bitcast_multiply_fusion) | copy-start | bytes 737284
  243.6 1.6 copy-start.12
  243.6 1.6 copy-start.22
  245.2 1.6 copy-start.1
  245.2 2.1 copy-start.7
  245.2 2.1 copy-start.9
  248.6 26.0 %all-to-all-start.2 = ((bf16[4,2,128,128]{3,1,0,2:T(2,128)(2,1)}), bf16[4,2,128,128]{3,1,0,2:T(2,128)(2,1)S(1)}, u32[]{:S(2)}, u32[]{:S(2)}) async-start(bf16[4,2,128,128]{3,1,0,2:T(2,128)(2,1)} %copy.53), calls=%async_computation.2 | async-start | bytes 524288 | tf_op jit(solution)/shard_map/all_to_all | solution.py:219
  252.6 142.2 %all-reduce.4.cloned.1.call-start = ((), (), s32[]{:S(2)}) async-start(), calls=%async_computation.6 | async-start | bytes 245760 | tf_op jit(solution)/shard_map/psum | solution.py:24
  274.7 121.0 %copy-start.4 = (bf16[960,128]{1,0:T(8,128)(2,1)S(1)}, bf16[960,128]{1,0:T(8,128)(2,1)}, u32[]{:S(2)}) copy-start(bf16[960,128]{1,0:T(8,128)(2,1)} %copy-done.3) | copy-start | bytes 737284
  279.9 128.1 %copy-start.10 = (bf16[4,120,128,1]{2,0,1,3:T(4,128)(2,1)S(1)}, bf16[4,120,128,1]{2,0,1,3:T(4,128)(2,1)}, u32[]{:S(2)}) copy-start(bf16[4,120,128,1]{2,0,1,3:T(4,128)(2,1)} %get-tuple-element.227) | copy-start | bytes 368644
  279.9 114.9 %all-to-all-start.4 = ((bf16[4,128,192]{1,2,0:T(8,128)(2,1)}), bf16[4,128,192]{1,2,0:T(8,128)(2,1)S(1)}, u32[]{:S(2)}, u32[]{:S(2)}) async-start(bf16[4,128,192]{1,2,0:T(8,128)(2,1)} %bitcast.55), calls=%async_computation.4 | async-start | bytes 393216 | tf_op jit(solution)/shard_map/all_to_all | solution.py:36
  284.2 169.4 %all-reduce.6.cloned.1.call-start = ((), (), s32[]{:S(2)}) async-start(), calls=%async_computation.7 | async-start | bytes 245760 | tf_op jit(solution)/shard_map/psum | solution.py:24
  394.8 87.8 %all-gather.5.cloned.1.call-start = ((), (), s32[]{:S(2)}) async-start(), calls=%async_computation.9 | async-start | bytes 1622016 | tf_op jit(solution)/shard_map/all_gather | solution.py:41
  395.6 32.6 %copy-start.11 = (f32[1,4,240,128]{3,2,1,0:T(8,128)S(1)}, f32[1,4,240,128]{3,2,1,0:T(8,128)}, u32[]{:S(2)}) copy-start(f32[1,4,240,128]{3,2,1,0:T(8,128)} %get-tuple-element.222) | copy-start | bytes 1474564
  395.6 32.6 %copy-start.14 = (bf16[1,1,4,240,128]{4,3,2,1,0:T(8,128)(2,1)S(1)}, bf16[1,1,4,240,128]{4,3,2,1,0:T(8,128)(2,1)}, u32[]{:S(2)}) copy-start(bf16[1,1,4,240,128]{4,3,2,1,0:T(8,128)(2,1)} %param.9) | copy-start | bytes 737284
  395.6 32.6 %copy-start.15 = (bf16[1,4,240,128]{3,2,1,0:T(8,128)(2,1)S(1)}, bf16[1,4,240,128]{3,2,1,0:T(8,128)(2,1)}, u32[]{:S(2)}) copy-start(bf16[1,4,240,128]{3,2,1,0:T(8,128)(2,1)} %get-tuple-element.220) | copy-start | bytes 737284
  395.6 32.6 %copy-start.23 = (bf16[1,768,128]{2,1,0:T(8,128)(2,1)S(1)}, bf16[1,768,128]{2,1,0:T(8,128)(2,1)}, u32[]{:S(2)}) copy-start(bf16[1,768,128]{2,1,0:T(8,128)(2,1)} %param.13) | copy-start | bytes 589828
  395.6 155.1 %all-gather.7.cloned.1.call-start = ((), (), s32[]{:S(2)}) async-start(), calls=%async_computation.10 | async-start | bytes 1622016 | tf_op jit(solution)/shard_map/all_gather | solution.py:41
  409.2 42.5 %all-to-all-start.3 = ((bf16[128,2,4,128]{3,1,2,0:T(2,128)(2,1)}), bf16[128,2,4,128]{3,1,2,0:T(2,128)(2,1)S(1)}, u32[]{:S(2)}, u32[]{:S(2)}) async-start(bf16[128,2,4,128]{3,1,2,0:T(2,128)(2,1)} %copy.57), calls=%async_computation.3 | async-start | bytes 524288 | tf_op jit(solution)/shard_map/all_to_all | solution.py:241
  427.9 125.1 %all-reduce.8.cloned.1.call-start = ((), (), s32[]{:S(2)}) async-start(), calls=%async_computation.8 | async-start | bytes 245760 | tf_op jit(solution)/shard_map/psum | solution.py:24
  428.2 23.9 %copy-start.17 = (bf16[240,128]{1,0:T(8,128)(2,1)S(1)}, bf16[240,128]{1,0:T(8,128)(2,1)}, u32[]{:S(2)}) copy-start(bf16[240,128]{1,0:T(8,128)(2,1)} %copy-done.16) | copy-start | bytes 184324
  428.2 23.9 %copy-start.19 = (bf16[240,128]{1,0:T(8,128)(2,1)S(1)}, bf16[240,128]{1,0:T(8,128)(2,1)}, u32[]{:S(2)}) copy-start(bf16[240,128]{1,0:T(8,128)(2,1)} %copy-done.18) | copy-start | bytes 184324
  429.3 24.3 %collective-permute-start = (bf16[1,1,4,240,128]{4,3,2,1,0:T(8,128)(2,1)S(1)}, bf16[1,1,4,240,128]{4,3,2,1,0:T(8,128)(2,1)S(1)}, u32[]{:S(2)}, u32[]{:S(2)}) collective-permute-start(bf16[1,1,4,240,128]{4,3,2,1,0:T(8,128)(2,1)S(1)} %multiply_convert_fusion.5), channel_id=1, source_target_pairs={{0,128},{128,256},{256,384},{1,129},{129,257},{257,385},{2,130},{1... | collective-permute-start | bytes 737288 | tf_op jit(solution)/shard_map/ppermute | solution.py:19
  452.3 8.9 %collective-permute-start.1 = (bf16[1,1,4,240,128]{4,3,2,1,0:T(8,128)(2,1)S(1)}, bf16[1,1,4,240,128]{4,3,2,1,0:T(8,128)(2,1)S(1)}, u32[]{:S(2)}, u32[]{:S(2)}) collective-permute-start(bf16[1,1,4,240,128]{4,3,2,1,0:T(8,128)(2,1)S(1)} %fusion.18), channel_id=1, source_target_pairs={{128,0},{256,128},{384,256},{129,1},{257,129},{385,257},{130,2},{2... | collective-permute-start | bytes 737288 | tf_op jit(solution)/shard_map/ppermute | solution.py:19
Sparse Core Ops, SparseCore 0:
  277.9 116.8 all-reduce.3
  397.9 45.9 all-reduce.5
  453.8 46.9 all-reduce.7
Sparse Core Ops, SparseCore 1:
  397.9 84.6 all-gather.4
  485.2 65.5 all-gather.6
where the time goes:
time: 565 us; the launch traced here: 563 us
  waiting for transfers between devices  275 us (49%)
  local copies, waits for them, and re-layouts  81.9 us (14%)
  loops' own time  80.9 us (14%)
  starting transfers between devices  60.8 us (11%)
  other arithmetic  27.5 us (5%)
  between operations  15.8 us (3%)
  matrix products  11.8 us (2%)
  blocking collectives  8.99 us (2%)
    psum x3, waiting for transfers between devices, one_axis_at_a_time(): shard = lax.psum(shard, axis)  111 us
    all_gather x2, waiting for transfers between devices, total_of_pieces(): return lax.all_gather(shard, axis).astype(jnp.float32).sum(0)  86.1 us
    another operation x1, loops' own time, legendre(): lax.scan(advance, (zero_rows, zero_rows), jnp.arange(cycles, dtype=jnp.in...  80.9 us
    dynamic_slice x120, local copies, waits for them, and re-layouts, legendre(): lax.scan(advance, (zero_rows, zero_rows), jnp.arange(cycles, dtype=jnp.in...  70.4 us
    all_to_all x1, waiting for transfers between devices, joint_cycles(): return lax.all_to_all(values, SP, split_axis=1, concat_axis=3, tiled=True)  32.4 us
    all_to_all x1, waiting for transfers between devices, on_device(): lax.all_to_all(grad_coeffs, SP, split_axis=0, concat_axis=2, tiled=True)  19.4 us
    all_to_all x1, waiting for transfers between devices, on_device(): lax.all_to_all(grad_values, SP, split_axis=2, concat_axis=0, tiled=True)  19.3 us
    all_to_all x1, starting transfers between devices, on_device(): lax.all_to_all(grad_coeffs, SP, split_axis=0, concat_axis=2, tiled=True)  18.6 us
  transfers between devices with their start and end apart: 12, of which 7 were waited for; matrix products, arithmetic and copies ran while one was open for 18% of the time, Pallas kernels for 0%

commit v1 on v0

--- a/solution.py
+++ b/solution.py
@@ -21,7 +21,7 @@
 
 def one_axis_at_a_time(shard, axes):
     for axis in axes:
-        shard = lax.psum(shard, axis)
+        shard = jnp.sum(lax.all_gather(shard, axis), axis=0)
     return shard
 
 

time: 565 us -> 501 us (0.89)
  waiting for transfers between devices: 275 us -> 200 us
  blocking collectives: 8.99 us -> 39.7 us
  starting transfers between devices: 60.8 us -> 44.3 us
    psum x3 -> x0, waiting for transfers between devices: 111 us -> none  [one_axis_at_a_time(): shard = lax.psum(shard, axis)]
    all_gather x0 -> x1, waiting for transfers between devices: none -> 59.2 us  [one_axis_at_a_time(): shard = jnp.sum(lax.all_gather(shard, axis), axis=0)]
    all_gather x2, waiting for transfers between devices: 86.1 us -> 61.4 us  [total_of_pieces(): return lax.all_gather(shard, axis).astype(jnp.float32).sum(0)]
    all_gather x0 -> x2, blocking collectives: none -> 22.9 us  [one_axis_at_a_time(): shard = jnp.sum(lax.all_gather(shard, axis), axis=0)]
    all_to_all x1, starting transfers between devices: 18.6 us -> 4.06 us  [on_device(): lax.all_to_all(grad_coeffs, SP, split_axis=0, concat_axis=2, tiled=True)]
    all_to_all x1 -> x2, blocking collectives: 8.99 us -> 16.7 us  [summed_on_arrival(): lax.all_to_all(blocks, axis, split_axis=0, concat_axis=0, tiled=True)]
  transfers between devices with their start and end apart: 12 -> 9, of which waited for: 7 -> 6; matrix products, arithmetic and copies ran while one was open for 18% -> 21% of each run, Pallas kernels for 0% -> 0%
where the time goes in v1:
time: 501 us; the launch traced here: 498 us
  waiting for transfers between devices  200 us (40%)
  loops' own time  80.9 us (16%)
  local copies, waits for them, and re-layouts  79.9 us (16%)
  starting transfers between devices  44.3 us (9%)
  blocking collectives  39.7 us (8%)
  other arithmetic  26.2 us (5%)
  between operations  14.3 us (3%)
  matrix products  12.7 us (3%)
    another operation x1, loops' own time, legendre(): lax.scan(advance, (zero_rows, zero_rows), jnp.arange(cycles, dtype=jnp.in...  80.9 us
    dynamic_slice x120, local copies, waits for them, and re-layouts, legendre(): lax.scan(advance, (zero_rows, zero_rows), jnp.arange(cycles, dtype=jnp.in...  70.4 us
    all_gather x2, waiting for transfers between devices, total_of_pieces(): return lax.all_gather(shard, axis).astype(jnp.float32).sum(0)  61.4 us
    all_gather x1, waiting for transfers between devices, one_axis_at_a_time(): shard = jnp.sum(lax.all_gather(shard, axis), axis=0)  59.2 us
    all_to_all x1, waiting for transfers between devices, joint_cycles(): return lax.all_to_all(values, SP, split_axis=1, concat_axis=3, tiled=True)  33.4 us
    all_to_all x1, waiting for transfers between devices, on_device(): lax.all_to_all(grad_values, SP, split_axis=2, concat_axis=0, tiled=True)  23.7 us
    all_gather x2, blocking collectives, one_axis_at_a_time(): shard = jnp.sum(lax.all_gather(shard, axis), axis=0)  22.9 us
    all_to_all x1, starting transfers between devices, joint_orders(): return lax.all_to_all(coeffs, SP, split_axis=3, concat_axis=1, tiled=True)  16.7 us
  transfers between devices with their start and end apart: 9, of which 6 were waited for; matrix products, arithmetic and copies ran while one was open for 21% of the time, Pallas kernels for 0%

profile of v1, /device:TPU:1, one launch (start us, length us, event | category | flops | bytes accessed | tf_op | source)
XLA Modules:
  0.0 497.8 jit_solution(9793673570980283473)
XLA Ops:
  8.4 1.4 convolution_convert_fusion.1
  9.8 1.3 copy.46
  11.1 16.7 %all-to-all-start = ((bf16[2,4,2,128,128]{4,2,1,0,3:T(2,128)(2,1)}), bf16[2,4,2,128,128]{4,2,1,0,3:T(2,128)(2,1)S(1)}, u32[]{:S(2)}, u32[]{:S(2)}) async-start(bf16[2,4,2,128,128]{4,2,1,0,3:T(2,128)(2,1)} %copy.46), calls=%async_computation | async-start | bytes 1048576 | tf_op jit(solution)/shard_map/all_to_all | solution.py:123
  28.2 164.7 %while.18 = (s32[]{:T(128)}, f32[4,128]{1,0:T(4,128)S(1)}, f32[4,128]{1,0:T(4,128)S(1)}, f32[120,4,128]{2,1,0:T(4,128)S(1)}, s32[120]{0:T(128)S(1)}, /*index=5*/...) while((s32[]{:T(128)}, f32[4,128]{1,0:T(4,128)S(1)}, ...), condition=%wide.region_1.2_spmd.clone, body=%wide.region_0.1_spmd.clone.sunk | while | flops 4654 | bytes 14747 | solution.py:90
  32.3 0.6 dynamic_slice.23
  52.9 0.6 dynamic_slice.23
  58.4 0.6 dynamic_slice.23
  79.0 0.6 dynamic_slice.23
  84.4 0.6 dynamic_slice.23
  105.0 0.6 dynamic_slice.23
  110.5 0.6 dynamic_slice.23
  131.1 0.6 dynamic_slice.23
  136.6 0.6 dynamic_slice.23
  193.0 0.8 fusion.54
  194.9 1.1 copy.50
  196.0 12.2 %all-to-all-start.1 = ((bf16[2,128,2,4,128]{4,2,0,3,1:T(2,128)(2,1)}), bf16[2,128,2,4,128]{4,2,0,3,1:T(2,128)(2,1)S(1)}, u32[]{:S(2)}, u32[]{:S(2)}) async-start(bf16[2,128,2,4,128]{4,2,0,3,1:T(2,128)(2,1)} %copy.50), calls=%async_computation.1 | async-start | bytes 1048576 | tf_op jit(solution)/shard_map/all_to_all | solution.py:127
  208.4 33.4 %all-to-all-done.1 = bf16[2,128,2,4,128]{4,2,0,3,1:T(2,128)(2,1)S(1)} async-done(((bf16[2,128,2,4,128]{4,2,0,3,1:T(2,128)(2,1)}), bf16[2,128,2,4,128]{4,2,0,3,1:T(2,128)(2,1)S(1)}, u32[]{:S(2)}, u32[]{:S(2)}) %all-to-all-start.1) | async-done | bytes 524320 | tf_op jit(solution)/shard_map/all_to_all | solution.py:127
  242.6 1.0 fusion.76
  244.2 1.4 fusion.7
  246.4 9.2 %all_to_all.76 = bf16[4,128,192]{1,2,0:T(8,128)(2,1)S(1)} all-to-all(bf16[4,128,192]{1,2,0:T(8,128)(2,1)S(1)} %bitcast.187), channel_id=1, replica_groups=mesh['pipe'=4,'sp_0'=16,'sp_1'=2,'dp'=4] {'dp'}, dimensions={0} | all-to-all | bytes 393216 | tf_op jit(solution)/shard_map/all_to_all | solution.py:36
  255.6 0.7 reduce_sum.87
  256.7 2.7 fusion.16
  259.3 7.5 %all_to_all.77 = bf16[4,192,128]{2,1,0:T(8,128)(2,1)S(1)} all-to-all(bf16[4,192,128]{2,1,0:T(8,128)(2,1)S(1)} %bitcast.197), channel_id=1, replica_groups=mesh['pipe'=4,'sp_0'=16,'sp_1'=2,'dp'=4] {'dp'}, dimensions={0} | all-to-all | bytes 393216 | tf_op jit(solution)/shard_map/all_to_all | solution.py:36
  266.9 0.6 reduce_sum.89
  268.1 1.1 convolution_convert_fusion.3
  269.3 1.0 copy.53
  270.2 6.6 %all-to-all-start.2 = ((bf16[4,2,128,128]{3,1,0,2:T(2,128)(2,1)}), bf16[4,2,128,128]{3,1,0,2:T(2,128)(2,1)S(1)}, u32[]{:S(2)}, u32[]{:S(2)}) async-start(bf16[4,2,128,128]{3,1,0,2:T(2,128)(2,1)} %copy.53), calls=%async_computation.2 | async-start | bytes 524288 | tf_op jit(solution)/shard_map/all_to_all | solution.py:219
  276.9 23.7 %all-to-all-done.2 = bf16[4,2,128,128]{3,1,0,2:T(2,128)(2,1)S(1)} async-done(((bf16[4,2,128,128]{3,1,0,2:T(2,128)(2,1)}), bf16[4,2,128,128]{3,1,0,2:T(2,128)(2,1)S(1)}, u32[]{:S(2)}, u32[]{:S(2)}) %all-to-all-start.2) | async-done | bytes 262176 | tf_op jit(solution)/shard_map/all_to_all | solution.py:219
  300.7 1.1 convolution_bitcast_fusion.3
  301.9 0.7 pad_maximum_fusion.2
  302.9 0.9 copy.57
  303.8 4.1 all-to-all-start.3
  307.9 2.1 fusion.14
  310.1 3.3 collective-permute-start
  313.4 14.8 %all-to-all-done.3 = bf16[128,2,4,128]{3,1,2,0:T(2,128)(2,1)S(1)} async-done(((bf16[128,2,4,128]{3,1,2,0:T(2,128)(2,1)}), bf16[128,2,4,128]{3,1,2,0:T(2,128)(2,1)S(1)}, u32[]{:S(2)}, u32[]{:S(2)}) %all-to-all-start.3) | async-done | bytes 262176 | tf_op jit(solution)/shard_map/all_to_all | solution.py:241
  328.7 1.3 collective-permute-start.1
  330.0 7.3 %collective-permute-done.1 = bf16[1,1,4,240,128]{4,3,2,1,0:T(8,128)(2,1)} collective-permute-done((bf16[1,1,4,240,128]{4,3,2,1,0:T(8,128)(2,1)S(1)}, bf16[1,1,4,240,128]{4,3,2,1,0:T(8,128)(2,1)}, u32[]{:S(2)}, u32[]{:S(2)}) %collective-permute-start.1) | collective-permute-done | bytes 245792 | tf_op jit(solution)/shard_map/ppermute | solution.py:19
  337.4 1.7 convert_bitcast_fusion
  339.7 61.4 %all-gather.11.cloned.1.call-done = bf16[6144,128]{1,0:T(8,128)(2,1)} async-done(((bf16[192,128]{1,0:T(8,128)(2,1)}), bf16[6144,128]{1,0:T(8,128)(2,1)}) %all-gather.11.cloned.1.call-update) | async-done | bytes 1572880 | tf_op jit(solution)/shard_map/all_gather | solution.py:41
  401.1 2.3 convert_reduce_fusion
  403.3 1.1 bitcast_reduce_fusion
  404.4 59.2 %all-gather.13.cloned.1.call-done = f32[32,120,128]{2,1,0:T(8,128)} async-done(((f32[2,120,128]{2,1,0:T(8,128)}), f32[32,120,128]{2,1,0:T(8,128)}) %all-gather.13.cloned.1.call-update) | async-done | bytes 1966096 | tf_op jit(solution)/shard_map/all_gather | solution.py:24
  463.7 1.6 reduce_sum.93
  465.3 11.8 %all-gather.3 = f32[4,120,128]{2,1,0:T(8,128)S(1)} all-gather(f32[2,120,128]{2,1,0:T(8,128)S(1)} %reduce_sum.93), channel_id=5, replica_groups=mesh['pipe'=4,'sp_0'=16,'sp_1'=2,'dp'=4] {'sp_1'}, dimensions={0}, use_global_device_ids=true | all-gather | bytes 368640 | tf_op jit(solution)/shard_map/all_gather | solution.py:24
  477.2 11.1 %all-gather.4 = f32[8,120,128]{2,1,0:T(8,128)S(1)} all-gather(f32[2,120,128]{2,1,0:T(8,128)S(1)} %reduce_sum.94), channel_id=6, replica_groups=mesh['pipe'=4,'sp_0'=16,'sp_1'=2,'dp'=4] {'dp'}, dimensions={0}, use_global_device_ids=true | all-gather | bytes 614400 | tf_op jit(solution)/shard_map/all_gather | solution.py:24
  488.3 0.7 reduce_sum.95
  489.0 0.7 copy.99
  489.6 1.7 copy.100
  (559 shorter events, 86.0 us)
Async XLA Ops:
  7.2 236.5 %copy-start = (bf16[1,128,768]{2,1,0:T(8,128)(2,1)S(1)}, bf16[1,128,768]{2,1,0:T(8,128)(2,1)}, u32[]{:S(2)}) copy-start(bf16[1,128,768]{2,1,0:T(8,128)(2,1)} %param.12) | copy-start | bytes 589828
  7.2 20.9 %copy-start.17 = (s32[128]{0:T(128)S(1)}, s32[128]{0:T(128)}, u32[]{:S(2)}) copy-start(s32[128]{0:T(128)} %param.15) | copy-start | bytes 1540
  7.2 185.8 %copy-start.16 = (f32[1,2,120,128]{3,2,1,0:T(8,128)S(1)}, f32[1,2,120,128]{3,2,1,0:T(8,128)}, u32[]{:S(2)}) copy-start(f32[1,2,120,128]{3,2,1,0:T(8,128)} %param.14) | copy-start | bytes 368644
  7.8 0.6 copy-start.12
  7.8 2.0 copy-start.14
  7.8 234.5 %copy-start.4 = (bf16[240,128]{1,0:T(8,128)(2,1)}, bf16[240,128]{1,0:T(8,128)(2,1)S(1)}, u32[]{:S(2)}) copy-start(bf16[240,128]{1,0:T(8,128)(2,1)S(1)} %get-tuple-element.233) | copy-start | bytes 184324
  7.8 234.5 %copy-start.5 = (bf16[240,128]{1,0:T(8,128)(2,1)}, bf16[240,128]{1,0:T(8,128)(2,1)S(1)}, u32[]{:S(2)}) copy-start(bf16[240,128]{1,0:T(8,128)(2,1)S(1)} %get-tuple-element.234) | copy-start | bytes 184324
  11.1 182.7 %all-to-all-start = ((bf16[2,4,2,128,128]{4,2,1,0,3:T(2,128)(2,1)}), bf16[2,4,2,128,128]{4,2,1,0,3:T(2,128)(2,1)S(1)}, u32[]{:S(2)}, u32[]{:S(2)}) async-start(bf16[2,4,2,128,128]{4,2,1,0,3:T(2,128)(2,1)} %copy.46), calls=%async_computation | async-start | bytes 1048576 | tf_op jit(solution)/shard_map/all_to_all | solution.py:123
  194.0 14.2 %copy-start.2 = (bf16[1,1,4,240,128]{4,3,2,1,0:T(8,128)(2,1)S(1)}, bf16[1,1,4,240,128]{4,3,2,1,0:T(8,128)(2,1)}, u32[]{:S(2)}) copy-start(bf16[1,1,4,240,128]{4,3,2,1,0:T(8,128)(2,1)} %param.11) | copy-start | bytes 737284
  194.8 47.7 %copy-start.3 = (bf16[1,1,4,240,128]{4,3,2,1,0:T(8,128)(2,1)S(1)}, bf16[1,1,4,240,128]{4,3,2,1,0:T(8,128)(2,1)}, u32[]{:S(2)}) copy-start(bf16[1,1,4,240,128]{4,3,2,1,0:T(8,128)(2,1)} %param.10) | copy-start | bytes 737284
  194.9 47.7 %copy-start.8 = (bf16[1,1,4,240,128]{4,3,2,1,0:T(8,128)(2,1)S(1)}, bf16[1,1,4,240,128]{4,3,2,1,0:T(8,128)(2,1)}, u32[]{:S(2)}) copy-start(bf16[1,1,4,240,128]{4,3,2,1,0:T(8,128)(2,1)} %param.9) | copy-start | bytes 737284
  196.0 45.7 %all-to-all-start.1 = ((bf16[2,128,2,4,128]{4,2,0,3,1:T(2,128)(2,1)}), bf16[2,128,2,4,128]{4,2,0,3,1:T(2,128)(2,1)S(1)}, u32[]{:S(2)}, u32[]{:S(2)}) async-start(bf16[2,128,2,4,128]{4,2,0,3,1:T(2,128)(2,1)} %copy.50), calls=%async_computation.1 | async-start | bytes 1048576 | tf_op jit(solution)/shard_map/all_to_all | solution.py:127
  208.2 129.2 %all-gather.9.cloned.1.call-start = ((), (), s32[]{:S(2)}) async-start(), calls=%async_computation.6 | async-start | bytes 1622016 | tf_op jit(solution)/shard_map/all_gather | solution.py:41
  242.6 1.6 copy-start.18
  244.2 1.6 copy-start.1
  256.2 144.8 %all-gather.11.cloned.1.call-start = ((), (), s32[]{:S(2)}) async-start(), calls=%async_computation.7 | async-start | bytes 1622016 | tf_op jit(solution)/shard_map/all_gather | solution.py:41
  268.1 34.5 %copy-start.6 = (bf16[4,120,128,1]{2,0,1,3:T(4,128)(2,1)S(1)}, bf16[4,120,128,1]{2,0,1,3:T(4,128)(2,1)}, u32[]{:S(2)}) copy-start(bf16[4,120,128,1]{2,0,1,3:T(4,128)(2,1)} %get-tuple-element.227) | copy-start | bytes 368644
  270.2 30.4 %all-to-all-start.2 = ((bf16[4,2,128,128]{3,1,0,2:T(2,128)(2,1)}), bf16[4,2,128,128]{3,1,0,2:T(2,128)(2,1)S(1)}, u32[]{:S(2)}, u32[]{:S(2)}) async-start(bf16[4,2,128,128]{3,1,0,2:T(2,128)(2,1)} %copy.53), calls=%async_computation.2 | async-start | bytes 524288 | tf_op jit(solution)/shard_map/all_to_all | solution.py:219
  276.8 31.1 %copy-start.7 = (f32[1,4,240,128]{3,2,1,0:T(8,128)S(1)}, f32[1,4,240,128]{3,2,1,0:T(8,128)}, u32[]{:S(2)}) copy-start(f32[1,4,240,128]{3,2,1,0:T(8,128)} %get-tuple-element.222) | copy-start | bytes 1474564
  276.8 31.1 %copy-start.9 = (bf16[1,1,4,240,128]{4,3,2,1,0:T(8,128)(2,1)S(1)}, bf16[1,1,4,240,128]{4,3,2,1,0:T(8,128)(2,1)}, u32[]{:S(2)}) copy-start(bf16[1,1,4,240,128]{4,3,2,1,0:T(8,128)(2,1)} %param.9) | copy-start | bytes 737284
  276.8 186.9 %all-gather.13.cloned.1.call-start = ((), (), s32[]{:S(2)}) async-start(), calls=%async_computation.8 | async-start | bytes 2088960 | tf_op jit(solution)/shard_map/all_gather | solution.py:24
  303.8 24.4 %all-to-all-start.3 = ((bf16[128,2,4,128]{3,1,2,0:T(2,128)(2,1)}), bf16[128,2,4,128]{3,1,2,0:T(2,128)(2,1)S(1)}, u32[]{:S(2)}, u32[]{:S(2)}) async-start(bf16[128,2,4,128]{3,1,2,0:T(2,128)(2,1)} %copy.57), calls=%async_computation.3 | async-start | bytes 524288 | tf_op jit(solution)/shard_map/all_to_all | solution.py:241
  307.9 20.6 %copy-start.13 = (bf16[240,128]{1,0:T(8,128)(2,1)S(1)}, bf16[240,128]{1,0:T(8,128)(2,1)}, u32[]{:S(2)}) copy-start(bf16[240,128]{1,0:T(8,128)(2,1)} %copy-done.12) | copy-start | bytes 184324
  307.9 20.6 %copy-start.15 = (bf16[240,128]{1,0:T(8,128)(2,1)S(1)}, bf16[240,128]{1,0:T(8,128)(2,1)}, u32[]{:S(2)}) copy-start(bf16[240,128]{1,0:T(8,128)(2,1)} %copy-done.14) | copy-start | bytes 184324
  310.1 19.9 %collective-permute-start = (bf16[1,1,4,240,128]{4,3,2,1,0:T(8,128)(2,1)S(1)}, bf16[1,1,4,240,128]{4,3,2,1,0:T(8,128)(2,1)S(1)}, u32[]{:S(2)}, u32[]{:S(2)}) collective-permute-start(bf16[1,1,4,240,128]{4,3,2,1,0:T(8,128)(2,1)S(1)} %multiply_convert_fusion.5), channel_id=1, source_target_pairs={{0,128},{128,256},{256,384},{1,129},{129,257},{257,385},{2,130},{1... | collective-permute-start | bytes 737288 | tf_op jit(solution)/shard_map/ppermute | solution.py:19
  328.7 8.7 %collective-permute-start.1 = (bf16[1,1,4,240,128]{4,3,2,1,0:T(8,128)(2,1)S(1)}, bf16[1,1,4,240,128]{4,3,2,1,0:T(8,128)(2,1)}, u32[]{:S(2)}, u32[]{:S(2)}) collective-permute-start(bf16[1,1,4,240,128]{4,3,2,1,0:T(8,128)(2,1)S(1)} %fusion.18), channel_id=1, source_target_pairs={{128,0},{256,128},{384,256},{129,1},{257,129},{385,257},{130,2},{2... | collective-permute-start | bytes 737288 | tf_op jit(solution)/shard_map/ppermute | solution.py:19
  330.0 7.4 %copy-start.10 = (bf16[1,1,4,240,128]{4,3,2,1,0:T(8,128)(2,1)}, bf16[1,1,4,240,128]{4,3,2,1,0:T(8,128)(2,1)S(1)}, u32[]{:S(2)}) copy-start(bf16[1,1,4,240,128]{4,3,2,1,0:T(8,128)(2,1)S(1)} %collective-permute-done) | copy-start | bytes 737284
  404.4 84.5 %copy-start.11 = (bf16[1,1,4,240,128]{4,3,2,1,0:T(8,128)(2,1)S(1)}, bf16[1,1,4,240,128]{4,3,2,1,0:T(8,128)(2,1)}, u32[]{:S(2)}) copy-start(bf16[1,1,4,240,128]{4,3,2,1,0:T(8,128)(2,1)} %copy-done.10) | copy-start | bytes 737284
Sparse Core Ops, SparseCore 0:
  256.4 71.4 all-gather.8
  329.9 71.0 all-gather.10
  403.7 59.8 all-gather.12
